TPU v7x, 32 devices: a whole 2x2x4 slice. The times are simulated.
32 devices in a mesh: box: 8 (over y, x, core), dir: 4 (over z).
Axes of the slice: x: 2, y: 2, z: 4, core: 2. Of those that a mesh axis runs over, the one named last changes fastest.
Arguments:
- children: bfloat16 [8, 8, 128, 4, 512], P('box', None, 'dir'), may hold values from -6 to 6
- legendre: bfloat16 [512, 256, 128], P('dir'), may hold values from -0.5 to 0.5
- axial_angle: float32 [2, 256], replicated, may hold values from -3.140625 to 3.140625
- planar_angle: float32 [4, 256, 512], P(None, 'dir'), may hold values from -3.140625 to 3.140625
- translator: bfloat16 [32, 2, 256, 512], P(None, None, 'dir'), may hold values from -0.8984375 to 0.8984375
- group_slot: int32 [8], P('box'), may hold values from 0 to 7, as said below
- source_list: int32 [8, 8], P('box'), may hold values from 0 to 7, as said below
- offset_list: int32 [8, 8], P('box'), may hold values from 0 to 31
- row_counts: int32 [8], P('box'), may hold values from 1 to 8
Outputs:
- incoming: bfloat16 [8, 256, 4, 512], P('box', 'dir')
Inputs may be any that keep to these rules, and one draw needn't show every extreme that they name: `group_slot`: each block of 1 row, one index of box, holds a permutation of that block's own row numbers. `source_list`: names a box group of the destination's own block of 1 row or of the block just before or just after it, never the destination itself.
All inputs are finite; a program needn't handle non-finite values.
Results may differ from a plain program's by a relative error of at most 0.0057.
Values may be sent and summed in bfloat16 or wider, within the bound.
A program may use at most 128 MiB of HBM per device.

v0:
```python
import functools
import math

import jax
import jax.numpy as jnp
import ml_dtypes
import numpy as np
from jax import lax
from jax.experimental import pallas as pl
from jax.experimental.pallas import tpu as pltpu
from jax.sharding import PartitionSpec as P

MESH = pl.DeviceIdType.MESH
F32 = jnp.float32
BF16 = jnp.bfloat16
LANES = 128


def extended(x, sides, width):
    for axis, dim in sides:
        peers, length = (lax.axis_size(axis), x.shape[dim])
        up = [(i, (i + 1) % peers) for i in range(peers - 1)]
        down = [(j, i) for i, j in up]
        last = lax.slice_in_dim(x, length - width, length, axis=dim)
        initial = lax.slice_in_dim(x, 0, width, axis=dim)
        before = lax.ppermute(last, axis, up)
        after = lax.ppermute(initial, axis, down)
        x = jnp.concatenate([before, x, after], axis=dim)
    return x


def dft_tables(length):
    samples = jnp.arange(length, dtype=jnp.int32)
    product = samples[:, None] * samples[None, :] % length
    phase = product.astype(jnp.float32) * (2.0 * math.pi / length)
    cosine = jnp.cos(phase) / math.sqrt(length)
    sine = jnp.sin(phase) / math.sqrt(length)
    return (cosine, sine)


def general(
    children,
    legendre,
    axial_angle,
    planar_angle,
    translator,
    group_slot,
    source_list,
    offset_list,
    row_counts,
):
    local_groups, kids, rows_in, comps, length = children.shape
    dir_count = lax.axis_size("dir")
    box_index = lax.axis_index("box")
    modes_local = legendre.shape[0]
    rows_out = legendre.shape[1] // dir_count
    cosine, sine = dft_tables(length)
    high = lax.Precision.HIGH
    values = children.astype(jnp.float32).reshape(local_groups, kids, rows_in, 2, 2, length)
    samples_real = values[..., 0, :]
    samples_imag = values[..., 1, :]
    spec_real = jnp.einsum("gkqpj,jm->mgkpq", samples_real, cosine, precision=high) + jnp.einsum(
        "gkqpj,jm->mgkpq", samples_imag, sine, precision=high
    )
    spec_imag = jnp.einsum("gkqpj,jm->mgkpq", samples_imag, cosine, precision=high) - jnp.einsum(
        "gkqpj,jm->mgkpq", samples_real, sine, precision=high
    )
    spectrum = jnp.stack([spec_real, spec_imag], axis=4)
    spectrum = spectrum.astype(jnp.bfloat16).reshape(
        1, length, local_groups * kids * comps * rows_in
    )
    received = lax.all_to_all(spectrum, "dir", split_axis=1, concat_axis=0, tiled=True)
    received = received.reshape(dir_count, modes_local, local_groups * kids * comps, rows_in)
    matrices = legendre.reshape(modes_local, dir_count, rows_out, dir_count, rows_in)
    interp = jnp.einsum("mabsq,smcq->macb", matrices, received, preferred_element_type=jnp.float32)
    interp = interp.reshape(modes_local, dir_count, local_groups, 2, 4, 2, 2, rows_out)
    angles = jnp.transpose(axial_angle.reshape(2, dir_count, rows_out), (1, 0, 2))
    axial_cos = jnp.cos(angles)[None, :, None, :, None, None, :]
    axial_sin = jnp.sin(angles)[None, :, None, :, None, None, :]
    part_real = interp[..., 0, :]
    part_imag = interp[..., 1, :]
    pairs_real = jnp.sum(part_real * axial_cos - part_imag * axial_sin, axis=3)
    pairs_imag = jnp.sum(part_real * axial_sin + part_imag * axial_cos, axis=3)
    pairs = jnp.stack([pairs_real, pairs_imag], axis=5)
    pairs = pairs.reshape(modes_local, dir_count, local_groups * 4 * 2 * 2 * rows_out)
    returned = lax.all_to_all(pairs, "dir", split_axis=1, concat_axis=0, tiled=True)
    combined = returned.reshape(length, local_groups, 4, 2, 2, rows_out)
    comb_real = combined[:, :, :, :, 0, :]
    comb_imag = combined[:, :, :, :, 1, :]
    field_real = jnp.einsum("mgxpb,mj->gxbpj", comb_real, cosine, precision=high) - jnp.einsum(
        "mgxpb,mj->gxbpj", comb_imag, sine, precision=high
    )
    field_imag = jnp.einsum("mgxpb,mj->gxbpj", comb_real, sine, precision=high) + jnp.einsum(
        "mgxpb,mj->gxbpj", comb_imag, cosine, precision=high
    )
    planar_cos = jnp.cos(planar_angle)[None, :, :, None, :]
    planar_sin = jnp.sin(planar_angle)[None, :, :, None, :]
    stored_real = jnp.sum(field_real * planar_cos - field_imag * planar_sin, axis=1)
    stored_imag = jnp.sum(field_real * planar_sin + field_imag * planar_cos, axis=1)
    stored = jnp.stack([stored_real, stored_imag], axis=3)
    stored = stored.reshape(local_groups, rows_out, comps, length).astype(jnp.bfloat16)
    local_slot = group_slot - box_index * local_groups
    placement = (local_slot[None, :] == jnp.arange(local_groups)[:, None]).astype(jnp.bfloat16)
    ordered = jnp.einsum("lk,kbcj->lbcj", placement, stored, preferred_element_type=jnp.float32)
    ordered = ordered.astype(jnp.bfloat16)
    window = extended(ordered, (("box", 0),), local_groups)
    relative = source_list - (box_index - 1) * local_groups
    near = (relative[..., None] == jnp.arange(window.shape[0])).astype(jnp.bfloat16)
    picked = jnp.einsum("glw,wbcj->glbcj", near, window, preferred_element_type=jnp.float32)
    picked = picked.reshape(local_groups, source_list.shape[1], rows_out, 2, 2, length)
    chosen = (offset_list[..., None] == jnp.arange(translator.shape[0])).astype(jnp.bfloat16)
    operator = jnp.einsum("glo,orbj->glrbj", chosen, translator, preferred_element_type=jnp.float32)
    live = (jnp.arange(source_list.shape[1])[None, :] < row_counts[:, None]).astype(jnp.float32)
    live = live[:, :, None, None, None]
    oper_real = operator[:, :, 0, :, None, :].astype(jnp.float32) * live
    oper_imag = operator[:, :, 1, :, None, :].astype(jnp.float32) * live
    picked_real = picked[..., 0, :].astype(jnp.float32)
    picked_imag = picked[..., 1, :].astype(jnp.float32)
    total_real = jnp.sum(oper_real * picked_real - oper_imag * picked_imag, axis=1)
    total_imag = jnp.sum(oper_real * picked_imag + oper_imag * picked_real, axis=1)
    result = jnp.stack([total_real, total_imag], axis=3).reshape(
        local_groups, rows_out, comps, length
    )
    return result.astype(jnp.bfloat16)


PARTS = 2
CHUNKS = 2 * PARTS


def forward_table(length, dirs):
    phase = np.outer(np.arange(length), np.arange(length)) % length * (2.0 * np.pi / length)
    cosine, sine = np.cos(phase), np.sin(phase)
    both = np.stack(
        [np.concatenate([cosine, sine], axis=1), np.concatenate([-sine, cosine], axis=1)], axis=0
    )
    both = both.reshape(2, dirs, PARTS, length // dirs // PARTS, 2 * length)
    both = both.transpose(2, 1, 0, 3, 4).reshape(PARTS, -1, 2 * length)
    return both.astype(ml_dtypes.bfloat16)


def inverse_table(length, dirs):
    phase = np.outer(np.arange(length), np.arange(length)) % length * (2.0 * np.pi / length)
    cosine, sine = np.cos(phase) / length, np.sin(phase) / length
    both = np.stack(
        [np.concatenate([cosine, sine], axis=1), np.concatenate([-sine, cosine], axis=1)], axis=0
    )
    both = both.reshape(2, dirs, PARTS, length // dirs // PARTS, 2 * length)
    both = both.transpose(2, 0, 1, 3, 4).reshape(PARTS, -1, 2 * length)
    return both.astype(ml_dtypes.bfloat16)


def fused(
    dirs,
    boxes,
    source_ref,
    offset_ref,
    count_ref,
    x_hbm,
    wf_hbm,
    axial_hbm,
    legendre_hbm,
    wi_hbm,
    planar_hbm,
    translator_hbm,
    out_ref,
    x_ref,
    wf_ref,
    axial_ref,
    legendre_ref,
    wi_ref,
    planar_ref,
    translator_ref,
    samples,
    send1,
    recv1,
    spread,
    pairs,
    send2,
    recv2,
    field,
    planar_cos,
    planar_sin,
    sums,
    stored,
    halo,
    local_sems,
    send1_sems,
    recv1_sems,
    send2_sems,
    recv2_sems,
    halo_send,
    halo_recv,
):
    me = lax.axis_index("dir")
    box = lax.axis_index("box")
    right, left = lax.rem(box + 1, boxes), lax.rem(box + boxes - 1, boxes)
    rows_out, length = planar_ref.shape[1:]
    modes = legendre_ref.shape[0] // PARTS
    rows_in = LANES // dirs
    slots = source_ref.shape[1]

    loads = [
        pltpu.make_async_copy(src, dst, local_sems.at[i])
        for i, (src, dst) in enumerate(
            (
                (legendre_hbm, legendre_ref),
                (planar_hbm, planar_ref),
                (translator_hbm, translator_ref),
                (wi_hbm, wi_ref),
                (axial_hbm, axial_ref),
                (x_hbm, x_ref),
                *((wf_hbm.at[i], wf_ref.at[i]) for i in range(PARTS)),
            )
        )
    ]
    barrier = pltpu.get_barrier_semaphore()
    for step in range(1, dirs):
        peer = lax.rem(me + step, dirs)
        pl.semaphore_signal(barrier, inc=1, device_id=(box, peer), device_id_type=MESH)
    for peer in (left, right):
        pl.semaphore_signal(barrier, inc=1, device_id=(peer, me), device_id_type=MESH)
    for i in (5, *range(6, 6 + PARTS), 1, 2, 0, 4, 3):
        loads[i].start()

    def out_copy(chunk, step):
        peer = lax.rem(me + step, dirs)
        return pltpu.make_async_remote_copy(
            src_ref=send1.at[chunk, peer],
            dst_ref=recv1.at[chunk, me],
            send_sem=send1_sems.at[chunk, step - 1],
            recv_sem=recv1_sems.at[chunk, step - 1],
            device_id=(box, peer),
            device_id_type=MESH,
        )

    def back_copy(chunk, step):
        peer = lax.rem(me + step, dirs)
        row = pl.multiple_of(me * modes, modes)
        return pltpu.make_async_remote_copy(
            src_ref=send2.at[chunk, peer],
            dst_ref=recv2.at[chunk, :, pl.ds(row, modes), :],
            send_sem=send2_sems.at[chunk, step - 1],
            recv_sem=recv2_sems.at[chunk, step - 1],
            device_id=(box, peer),
            device_id_type=MESH,
        )

    comps = LANES // rows_in
    to = lax.broadcasted_iota(jnp.int32, (LANES, LANES), 0)
    come = lax.broadcasted_iota(jnp.int32, (LANES, LANES), 1)
    order = ((to % rows_in) * comps + to // rows_in == come).astype(F32).astype(BF16)
    loads[5].wait()
    for k in range(x_ref.shape[0]):
        sorted_rows = jnp.dot(
            order, x_ref[k].reshape(LANES, length), preferred_element_type=F32
        ).astype(BF16)
        for c in range(comps):
            p, r = c // 2, c % 2
            row = (p * x_ref.shape[0] + k) * rows_in
            samples[row : row + rows_in, r * length : (r + 1) * length] = sorted_rows[
                c * rows_in : (c + 1) * rows_in
            ]
    pl.semaphore_wait(barrier, dirs + 1)
    cols = samples.shape[0] // 2

    for chunk in range(CHUNKS):
        p, part = chunk // PARTS, chunk % PARTS
        if p == 0:
            loads[6 + part].wait()
        spectrum = lax.dot_general(
            wf_ref[part],
            samples[p * cols : (p + 1) * cols],
            (((1,), (1,)), ((), ())),
            preferred_element_type=F32,
        )
        send1[chunk] = spectrum.astype(BF16).reshape(send1.shape[1:])
        for step in range(1, dirs):
            out_copy(chunk, step).start()
        recv1[chunk, me] = send1[chunk, me]

    loads[1].wait()
    for q in range(4):
        planar_cos[q] = jnp.cos(planar_ref[q])
        planar_sin[q] = jnp.sin(planar_ref[q])
    loads[2].wait()
    sums[...] = jnp.zeros_like(sums)

    def gather(slot, carry):
        source, op = source_ref[0, slot], offset_ref[0, slot]
        live = slot < count_ref[0]
        before = jnp.where(jnp.logical_and(live, source < box), 1.0, 0.0)
        after = jnp.where(jnp.logical_and(live, source > box), 1.0, 0.0)
        for r in range(2):
            tile = translator_ref[op, r].astype(F32)
            sums[0, r] += before * tile
            sums[1, r] += after * tile
        return carry

    lax.fori_loop(0, slots, gather, 0)

    loads[4].wait()
    kids = x_ref.shape[0]
    theta = axial_ref.shape[1]
    upper = lax.broadcasted_iota(jnp.int32, (kids, theta), 0) < kids // 2
    angle = jnp.where(upper, axial_ref[0:1], axial_ref[1:2])
    axial_cos, axial_sin = jnp.cos(angle), jnp.sin(angle)
    block = lax.broadcasted_iota(jnp.int32, (modes, LANES), 1) // rows_in
    half = lax.broadcasted_iota(jnp.int32, (modes, LANES), 1) < rows_out
    loads[0].wait()

    def interpolate(chunk, carry):
        for step in range(1, dirs):
            out_copy(chunk, step).wait_recv()
        for r in range(2):
            for g in range(kids // dirs):
                tiles = [
                    recv1[
                        chunk, s, r * modes : (r + 1) * modes, g * LANES : (g + 1) * LANES
                    ].astype(F32)
                    for s in range(dirs)
                ]
                for a in range(dirs):
                    out = tiles[a]
                    for s in range(dirs):
                        if s != a:
                            shift = ((s - a) * rows_in) % LANES
                            out = jnp.where(block == s, pltpu.roll(tiles[s], shift, 1), out)
                    spread[pl.ds(r * kids + g * dirs + a, modes, stride=2 * kids), :] = out
        first = lax.rem(chunk, PARTS) * modes

        def mode(i, inner):
            rows = spread[pl.ds(pl.multiple_of(i * 2 * kids, 2 * kids), 2 * kids), :]
            value = lax.dot_general(
                rows.astype(BF16),
                legendre_ref[first + i],
                (((1,), (1,)), ((), ())),
                preferred_element_type=F32,
            )
            real, imag = value[:kids], value[kids:]
            sum_real = real * axial_cos - imag * axial_sin
            sum_imag = real * axial_sin + imag * axial_cos
            both = jnp.where(
                upper,
                sum_real + pltpu.roll(sum_real, kids // 2, 0),
                sum_imag + pltpu.roll(sum_imag, kids // 2, 0),
            )
            for n in range(pairs.shape[0]):
                tile = pairs.at[n]
                tile[pl.ds(i, kids, stride=modes), :] = both[:, n * LANES : (n + 1) * LANES]
            return inner

        lax.fori_loop(0, modes, mode, 0, unroll=8)
        for n in range(pairs.shape[0]):
            for jr in range(4):
                row = ((jr % 2) * 4 + (jr // 2) * 2) * modes
                one = pairs[n, row : row + modes, :]
                two = pairs[n, row + modes : row + 2 * modes, :]
                low = jnp.where(half, one, pltpu.roll(two, rows_out, 1))
                high = jnp.where(half, pltpu.roll(one, rows_out, 1), two)
                send2[chunk, 2 * n, jr] = low.astype(BF16)
                send2[chunk, 2 * n + 1, jr] = high.astype(BF16)
        for step in range(1, dirs):
            back_copy(chunk, step).start()
        row = pl.multiple_of(me * modes, modes)
        recv2[chunk, :, pl.ds(row, modes), :] = send2[chunk, me]
        return carry

    lax.fori_loop(0, CHUNKS, interpolate, 0)

    loads[3].wait()
    moves = [
        [
            pltpu.make_async_remote_copy(
                src_ref=stored.at[p],
                dst_ref=halo.at[side, p],
                send_sem=halo_send.at[side, p],
                recv_sem=halo_recv.at[side, p],
                device_id=(peer, me),
                device_id_type=MESH,
            )
            for side, peer in enumerate((right, left))
        ]
        for p in range(2)
    ]
    for p in range(2):
        for part in range(PARTS):
            chunk = p * PARTS + part
            for step in range(1, dirs):
                back_copy(chunk, step).wait_recv()
            for j in range(2):
                rows = recv2[chunk, 2 * j : 2 * j + 2].reshape(-1, LANES)
                term = lax.dot_general(
                    rows, wi_ref[part], (((0,), (0,)), ((), ())), preferred_element_type=F32
                )
                field[j] = term if part == 0 else field[j] + term
        total_real, total_imag = 0.0, 0.0
        for q in range(4):
            cos, sin = planar_cos[q], planar_sin[q]
            rows = slice((q % 2) * rows_out, (q % 2 + 1) * rows_out)
            real, imag = field[q // 2, rows, :length], field[q // 2, rows, length:]
            total_real = total_real + (real * cos - imag * sin)
            total_imag = total_imag + (real * sin + imag * cos)
        stored[p, 0] = total_real.astype(BF16)
        stored[p, 1] = total_imag.astype(BF16)
        for move in moves[p]:
            move.start()
    for chunk in range(CHUNKS):
        for step in range(1, dirs):
            out_copy(chunk, step).wait_send()
            back_copy(chunk, step).wait_send()
    for p in range(2):
        for move in moves[p]:
            move.wait()
        real, imag = 0.0, 0.0
        for side in range(2):
            source_real = halo[side, p, 0].astype(F32)
            source_imag = halo[side, p, 1].astype(F32)
            real = real + (sums[side, 0] * source_real - sums[side, 1] * source_imag)
            imag = imag + (sums[side, 0] * source_imag + sums[side, 1] * source_real)
        out_ref[2 * p] = real.astype(BF16)
        out_ref[2 * p + 1] = imag.astype(BF16)


def shards(
    children,
    legendre,
    axial_angle,
    planar_angle,
    translator,
    group_slot,
    source_list,
    offset_list,
    row_counts,
):
    local_groups, kids, rows_in, comps, length = children.shape
    dirs = lax.axis_size("dir")
    boxes = lax.axis_size("box")
    modes_local, theta_out, theta_in = legendre.shape
    rows_out = theta_out // dirs
    fits = (
        local_groups == 1
        and dirs == 4
        and boxes > 2
        and kids == 8
        and comps == 4
        and theta_in == LANES
        and 2 * rows_out == LANES
        and modes_local == LANES
    )
    if not fits:
        return general(
            children,
            legendre,
            axial_angle,
            planar_angle,
            translator,
            group_slot,
            source_list,
            offset_list,
            row_counts,
        )
    rows = kids * 2 * rows_in
    forward = jnp.asarray(forward_table(length, dirs))
    modes = modes_local // PARTS
    vmem = pl.BlockSpec(memory_space=pltpu.VMEM)
    smem = pl.BlockSpec(memory_space=pltpu.SMEM)
    hbm = pl.BlockSpec(memory_space=pl.ANY)
    inverse = jnp.asarray(inverse_table(length, dirs))
    exchange = pltpu.SemaphoreType.DMA((CHUNKS, dirs - 1))
    out = pl.pallas_call(
        functools.partial(fused, dirs, boxes),
        out_shape=jax.ShapeDtypeStruct((comps, rows_out, length), BF16),
        in_specs=[smem] * 3 + [hbm] * 7,
        out_specs=vmem,
        scratch_shapes=[
            pltpu.VMEM(children.shape[1:], BF16),
            pltpu.VMEM(forward.shape, BF16),
            pltpu.VMEM(axial_angle.shape, F32),
            pltpu.VMEM(legendre.shape, BF16),
            pltpu.VMEM(inverse.shape, BF16),
            pltpu.VMEM(planar_angle.shape, F32),
            pltpu.VMEM(translator.shape, BF16),
            pltpu.VMEM((rows, 2 * length), BF16),
            pltpu.VMEM((CHUNKS, dirs, 2 * modes, rows // 2), BF16),
            pltpu.VMEM((CHUNKS, dirs, 2 * modes, rows // 2), BF16),
            pltpu.VMEM((modes * kids * 2, LANES), F32),
            pltpu.VMEM((theta_out // LANES, 8 * modes, LANES), F32),
            pltpu.VMEM((CHUNKS, dirs, 4, modes, LANES), BF16),
            pltpu.VMEM((CHUNKS, 4, length // PARTS, LANES), BF16),
            pltpu.VMEM((2, LANES, 2 * length), F32),
            pltpu.VMEM(planar_angle.shape, F32),
            pltpu.VMEM(planar_angle.shape, F32),
            pltpu.VMEM((2, 2, rows_out, length), F32),
            pltpu.VMEM((2, 2, rows_out, length), BF16),
            pltpu.VMEM((2, 2, 2, rows_out, length), BF16),
            pltpu.SemaphoreType.DMA((6 + PARTS,)),
            exchange,
            exchange,
            exchange,
            exchange,
            pltpu.SemaphoreType.DMA((2, 2)),
            pltpu.SemaphoreType.DMA((2, 2)),
        ],
        compiler_params=pltpu.CompilerParams(
            collective_id=0, has_side_effects=True, vmem_limit_bytes=63 * 1024 * 1024
        ),
    )(
        source_list,
        offset_list,
        row_counts,
        children[0],
        forward,
        axial_angle,
        legendre,
        inverse,
        planar_angle,
        translator,
    )
    return out.transpose(1, 0, 2)[None]


def solution(mesh):
    placed = (
        P("box", None, "dir", None, None),
        P("dir", None, None),
        P(),
        P(None, "dir", None),
        P(None, None, "dir", None),
        P("box"),
        P("box", None),
        P("box", None),
        P("box"),
    )
    return jax.shard_map(
        shards, mesh=mesh, in_specs=placed, out_specs=P("box", "dir", None, None), check_vma=False
    )
```

profile of v0, /device:TPU:1, one launch (start us, length us, event | category | flops | bytes accessed | tf_op | source)
XLA Modules:
  0.0 60.4 jit_solution(186496563413694102)
XLA Ops:
  0.7 57.9 %shard_map.100 = bf16[4,64,512]{2,1,0:T(8,128)(2,1)} custom-call(s32[1,8]{1,0:T(1,128)} %source_ref.1, s32[1,8]{1,0:T(1,128)} %offset_ref.1, s32[1]{0:T(128)S(6)} %copy.12.count_ref, bf16[8,32,4,512]{3,2,1,0:T(4,128)(2,1)} %bitcast.5, bf16[2,512,1024]{2,1,0:T(8,128)(2,1)} %constant.4.clone.wf_hbm, f32[2,256]{1,0:T(2,128)} %axial_hbm.1, ...), custom_call_target="tpu_custom_call" | custom-call | tf_op jit(solution)/shard_map/pallas_call | solution.py:471
  58.6 1.9 %copy.11 = bf16[1,64,4,512]{3,2,1,0:T(4,128)(2,1)} copy(bf16[1,64,4,512]{3,1,2,0:T(8,128)(2,1)} %bitcast.4) | data formatting | bytes 524288 | tf_op jit(solution)/shard_map/broadcast_in_dim | solution.py:520
where the time goes:
time: 60.6 us; the launch traced here: 60.4 us
  Pallas kernels  57.9 us (96%)
  local copies, waits for them, and re-layouts  1.86 us (3%)
  between operations  0.66 us (1%)
    pallas_call x1, Pallas kernels, shards(): pl.pallas_call(functools.partial(fused, dirs, boxes), out_shape=jax.Shape...  57.9 us
    broadcast_in_dim x1, local copies, waits for them, and re-layouts, shards(): return out.transpose(1, 0, 2)[None]  1.86 us

commit v1 on v0

--- a/solution.py
+++ b/solution.py
@@ -139,23 +139,21 @@
     return both.astype(ml_dtypes.bfloat16)
 
 
-def inverse_table(length, dirs):
+def inverse_table(length):
     phase = np.outer(np.arange(length), np.arange(length)) % length * (2.0 * np.pi / length)
     cosine, sine = np.cos(phase) / length, np.sin(phase) / length
-    both = np.stack(
+    both = np.concatenate(
         [np.concatenate([cosine, sine], axis=1), np.concatenate([-sine, cosine], axis=1)], axis=0
     )
-    both = both.reshape(2, dirs, PARTS, length // dirs // PARTS, 2 * length)
-    both = both.transpose(2, 0, 1, 3, 4).reshape(PARTS, -1, 2 * length)
     return both.astype(ml_dtypes.bfloat16)
 
 
 def fused(
     dirs,
     boxes,
-    source_ref,
-    offset_ref,
-    count_ref,
+    source_hbm,
+    offset_hbm,
+    count_hbm,
     x_hbm,
     wf_hbm,
     axial_hbm,
@@ -164,6 +162,9 @@
     planar_hbm,
     translator_hbm,
     out_ref,
+    source_ref,
+    offset_ref,
+    count_ref,
     x_ref,
     wf_ref,
     axial_ref,
@@ -178,13 +179,13 @@
     pairs,
     send2,
     recv2,
-    field,
     planar_cos,
     planar_sin,
     sums,
     stored,
     halo,
     local_sems,
+    index_sems,
     send1_sems,
     recv1_sems,
     send2_sems,
@@ -196,64 +197,69 @@
     box = lax.axis_index("box")
     right, left = lax.rem(box + 1, boxes), lax.rem(box + boxes - 1, boxes)
     rows_out, length = planar_ref.shape[1:]
-    modes = legendre_ref.shape[0] // PARTS
+    own = legendre_ref.shape[0]
+    modes = own // PARTS
     rows_in = LANES // dirs
     slots = source_ref.shape[1]
-
-    loads = [
-        pltpu.make_async_copy(src, dst, local_sems.at[i])
-        for i, (src, dst) in enumerate(
-            (
-                (legendre_hbm, legendre_ref),
-                (planar_hbm, planar_ref),
-                (translator_hbm, translator_ref),
-                (wi_hbm, wi_ref),
-                (axial_hbm, axial_ref),
-                (x_hbm, x_ref),
-                *((wf_hbm.at[i], wf_ref.at[i]) for i in range(PARTS)),
-            )
-        )
-    ]
+    peers = (me + 1 - 2 * lax.rem(me, 2), lax.rem(me + 2, 4), 3 - me)
+    order = (1, 2, 0)
+
     barrier = pltpu.get_barrier_semaphore()
-    for step in range(1, dirs):
-        peer = lax.rem(me + step, dirs)
+    for peer in peers:
         pl.semaphore_signal(barrier, inc=1, device_id=(box, peer), device_id_type=MESH)
     for peer in (left, right):
         pl.semaphore_signal(barrier, inc=1, device_id=(peer, me), device_id_type=MESH)
-    for i in (5, *range(6, 6 + PARTS), 1, 2, 0, 4, 3):
-        loads[i].start()
+
+    def load(src, dst, sem):
+        return pltpu.make_async_copy(src, dst, sem)
+
+    load_x = load(x_hbm, x_ref, local_sems.at[0])
+    load_wf = [load(wf_hbm.at[i], wf_ref.at[i], local_sems.at[1 + i]) for i in range(PARTS)]
+    at = 1 + PARTS
+    load_planar = load(planar_hbm, planar_ref, local_sems.at[at])
+    load_translator = load(translator_hbm, translator_ref, local_sems.at[at + 1])
+    load_legendre = load(legendre_hbm, legendre_ref, local_sems.at[at + 2])
+    load_axial = load(axial_hbm, axial_ref, local_sems.at[at + 3])
+    load_wi = load(wi_hbm, wi_ref, local_sems.at[at + 4])
+    load_index = [
+        load(src, dst, index_sems.at[i])
+        for i, (src, dst) in enumerate(
+            ((source_hbm, source_ref), (offset_hbm, offset_ref), (count_hbm, count_ref))
+        )
+    ]
+    for item in (load_x, *load_wf):
+        item.start()
 
     def out_copy(chunk, step):
-        peer = lax.rem(me + step, dirs)
         return pltpu.make_async_remote_copy(
-            src_ref=send1.at[chunk, peer],
+            src_ref=send1.at[chunk, peers[step]],
             dst_ref=recv1.at[chunk, me],
-            send_sem=send1_sems.at[chunk, step - 1],
-            recv_sem=recv1_sems.at[chunk, step - 1],
-            device_id=(box, peer),
+            send_sem=send1_sems.at[chunk, step],
+            recv_sem=recv1_sems.at[chunk, step],
+            device_id=(box, peers[step]),
             device_id_type=MESH,
         )
 
-    def back_copy(chunk, step):
-        peer = lax.rem(me + step, dirs)
-        row = pl.multiple_of(me * modes, modes)
+    place = pl.ds(pl.multiple_of(me * own, own), own)
+
+    def back_copy(p, h, step):
         return pltpu.make_async_remote_copy(
-            src_ref=send2.at[chunk, peer],
-            dst_ref=recv2.at[chunk, :, pl.ds(row, modes), :],
-            send_sem=send2_sems.at[chunk, step - 1],
-            recv_sem=recv2_sems.at[chunk, step - 1],
-            device_id=(box, peer),
+            src_ref=send2.at[p, h, peers[step]],
+            dst_ref=recv2.at[p, h, :, place, :],
+            send_sem=send2_sems.at[p, h, step],
+            recv_sem=recv2_sems.at[p, h, step],
+            device_id=(box, peers[step]),
             device_id_type=MESH,
         )
 
     comps = LANES // rows_in
     to = lax.broadcasted_iota(jnp.int32, (LANES, LANES), 0)
     come = lax.broadcasted_iota(jnp.int32, (LANES, LANES), 1)
-    order = ((to % rows_in) * comps + to // rows_in == come).astype(F32).astype(BF16)
-    loads[5].wait()
+    sorting = ((to % rows_in) * comps + to // rows_in == come).astype(F32).astype(BF16)
+    load_x.wait()
     for k in range(x_ref.shape[0]):
         sorted_rows = jnp.dot(
-            order, x_ref[k].reshape(LANES, length), preferred_element_type=F32
+            sorting, x_ref[k].reshape(LANES, length), preferred_element_type=F32
         ).astype(BF16)
         for c in range(comps):
             p, r = c // 2, c % 2
@@ -261,13 +267,12 @@
             samples[row : row + rows_in, r * length : (r + 1) * length] = sorted_rows[
                 c * rows_in : (c + 1) * rows_in
             ]
-    pl.semaphore_wait(barrier, dirs + 1)
     cols = samples.shape[0] // 2
 
     for chunk in range(CHUNKS):
         p, part = chunk // PARTS, chunk % PARTS
         if p == 0:
-            loads[6 + part].wait()
+            load_wf[part].wait()
         spectrum = lax.dot_general(
             wf_ref[part],
             samples[p * cols : (p + 1) * cols],
@@ -275,15 +280,25 @@
             preferred_element_type=F32,
         )
         send1[chunk] = spectrum.astype(BF16).reshape(send1.shape[1:])
-        for step in range(1, dirs):
-            out_copy(chunk, step).start()
+        if chunk == 0:
+            pl.semaphore_wait(barrier, dirs + 1)
+        out_copy(chunk, 1).start()
+        out_copy(chunk, 2).start()
+        if chunk == 0:
+            for item in (load_planar, *load_index, load_translator, load_axial, load_legendre, load_wi):
+                item.start()
+        if part == PARTS - 1:
+            for i in range(PARTS):
+                out_copy(p * PARTS + i, 0).start()
         recv1[chunk, me] = send1[chunk, me]
 
-    loads[1].wait()
+    load_planar.wait()
     for q in range(4):
         planar_cos[q] = jnp.cos(planar_ref[q])
         planar_sin[q] = jnp.sin(planar_ref[q])
-    loads[2].wait()
+    for item in load_index:
+        item.wait()
+    load_translator.wait()
     sums[...] = jnp.zeros_like(sums)
 
     def gather(slot, carry):
@@ -299,18 +314,26 @@
 
     lax.fori_loop(0, slots, gather, 0)
 
-    loads[4].wait()
+    load_axial.wait()
     kids = x_ref.shape[0]
     theta = axial_ref.shape[1]
     upper = lax.broadcasted_iota(jnp.int32, (kids, theta), 0) < kids // 2
     angle = jnp.where(upper, axial_ref[0:1], axial_ref[1:2])
     axial_cos, axial_sin = jnp.cos(angle), jnp.sin(angle)
     block = lax.broadcasted_iota(jnp.int32, (modes, LANES), 1) // rows_in
-    half = lax.broadcasted_iota(jnp.int32, (modes, LANES), 1) < rows_out
-    loads[0].wait()
-
-    def interpolate(chunk, carry):
-        for step in range(1, dirs):
+    load_legendre.wait()
+
+    def exchanged(tiles, a):
+        out = tiles[a]
+        for s in range(4):
+            if s != a:
+                shift = ((s - a) * rows_in) % LANES
+                out = jnp.where(block == s, pltpu.roll(tiles[s], shift, 1), out)
+        return out
+
+    def interpolate(p, part):
+        chunk = p * PARTS + part
+        for step in range(3):
             out_copy(chunk, step).wait_recv()
         for r in range(2):
             for g in range(kids // dirs):
@@ -321,13 +344,10 @@
                     for s in range(dirs)
                 ]
                 for a in range(dirs):
-                    out = tiles[a]
-                    for s in range(dirs):
-                        if s != a:
-                            shift = ((s - a) * rows_in) % LANES
-                            out = jnp.where(block == s, pltpu.roll(tiles[s], shift, 1), out)
-                    spread[pl.ds(r * kids + g * dirs + a, modes, stride=2 * kids), :] = out
-        first = lax.rem(chunk, PARTS) * modes
+                    spread[pl.ds(r * kids + g * dirs + a, modes, stride=2 * kids), :] = exchanged(
+                        tiles, a
+                    )
+        first = part * modes
 
         def mode(i, inner):
             rows = spread[pl.ds(pl.multiple_of(i * 2 * kids, 2 * kids), 2 * kids), :]
@@ -351,75 +371,82 @@
             return inner
 
         lax.fori_loop(0, modes, mode, 0, unroll=8)
+        rows = pl.ds(pl.multiple_of(first, modes), modes)
         for n in range(pairs.shape[0]):
-            for jr in range(4):
-                row = ((jr % 2) * 4 + (jr // 2) * 2) * modes
-                one = pairs[n, row : row + modes, :]
-                two = pairs[n, row + modes : row + 2 * modes, :]
-                low = jnp.where(half, one, pltpu.roll(two, rows_out, 1))
-                high = jnp.where(half, pltpu.roll(one, rows_out, 1), two)
-                send2[chunk, 2 * n, jr] = low.astype(BF16)
-                send2[chunk, 2 * n + 1, jr] = high.astype(BF16)
-        for step in range(1, dirs):
-            back_copy(chunk, step).start()
-        row = pl.multiple_of(me * modes, modes)
-        recv2[chunk, :, pl.ds(row, modes), :] = send2[chunk, me]
-        return carry
-
-    lax.fori_loop(0, CHUNKS, interpolate, 0)
-
-    loads[3].wait()
-    moves = [
-        [
-            pltpu.make_async_remote_copy(
-                src_ref=stored.at[p],
-                dst_ref=halo.at[side, p],
-                send_sem=halo_send.at[side, p],
-                recv_sem=halo_recv.at[side, p],
-                device_id=(peer, me),
-                device_id_type=MESH,
-            )
-            for side, peer in enumerate((right, left))
-        ]
-        for p in range(2)
-    ]
+            for r in range(2):
+                tiles = [
+                    pairs[n, (r * 4 + q) * modes : (r * 4 + q + 1) * modes, :] for q in range(4)
+                ]
+                for g in range(4):
+                    send2[p, g % 2, 2 * n + g // 2, r, rows] = exchanged(tiles, g).astype(BF16)
+
     for p in range(2):
-        for part in range(PARTS):
-            chunk = p * PARTS + part
-            for step in range(1, dirs):
-                back_copy(chunk, step).wait_recv()
-            for j in range(2):
-                rows = recv2[chunk, 2 * j : 2 * j + 2].reshape(-1, LANES)
-                term = lax.dot_general(
-                    rows, wi_ref[part], (((0,), (0,)), ((), ())), preferred_element_type=F32
-                )
-                field[j] = term if part == 0 else field[j] + term
+
+        def both_parts(part, carry, p=p):
+            interpolate(p, part)
+            return carry
+
+        lax.fori_loop(0, PARTS, both_parts, 0)
+        for h, step in ((0, 1), (1, 1), (0, 2), (1, 2), (0, 0), (1, 0)):
+            back_copy(p, h, step).start()
+        for h in range(2):
+            recv2[p, h, :, place, :] = send2[p, h, me]
+
+    load_wi.wait()
+    has = (box < boxes - 1, box > 0)
+
+    def move(p, h, side):
+        return pltpu.make_async_remote_copy(
+            src_ref=stored.at[p, h],
+            dst_ref=halo.at[side, p, h],
+            send_sem=halo_send.at[side, p, h],
+            recv_sem=halo_recv.at[side, p, h],
+            device_id=((right, left)[side], me),
+            device_id_type=MESH,
+        )
+
+    rows_half = rows_out // 2
+    pieces = [(p, h) for p in range(2) for h in range(2)]
+    for p, h in pieces:
+        for step in range(3):
+            back_copy(p, h, step).wait_recv()
+        field = lax.dot_general(
+            recv2[p, h].reshape(-1, LANES),
+            wi_ref[...],
+            (((0,), (0,)), ((), ())),
+            preferred_element_type=F32,
+        )
         total_real, total_imag = 0.0, 0.0
         for q in range(4):
-            cos, sin = planar_cos[q], planar_sin[q]
-            rows = slice((q % 2) * rows_out, (q % 2 + 1) * rows_out)
-            real, imag = field[q // 2, rows, :length], field[q // 2, rows, length:]
+            cos = planar_cos[q, h * rows_half : (h + 1) * rows_half]
+            sin = planar_sin[q, h * rows_half : (h + 1) * rows_half]
+            real = field[q * rows_half : (q + 1) * rows_half, :length]
+            imag = field[q * rows_half : (q + 1) * rows_half, length:]
             total_real = total_real + (real * cos - imag * sin)
             total_imag = total_imag + (real * sin + imag * cos)
-        stored[p, 0] = total_real.astype(BF16)
-        stored[p, 1] = total_imag.astype(BF16)
-        for move in moves[p]:
-            move.start()
-    for chunk in range(CHUNKS):
-        for step in range(1, dirs):
+        stored[p, h, 0] = total_real.astype(BF16)
+        stored[p, h, 1] = total_imag.astype(BF16)
+        for side in range(2):
+            pl.when(has[side])(move(p, h, side).start)
+    for step in range(3):
+        for chunk in range(CHUNKS):
             out_copy(chunk, step).wait_send()
-            back_copy(chunk, step).wait_send()
-    for p in range(2):
-        for move in moves[p]:
-            move.wait()
+        for p, h in pieces:
+            back_copy(p, h, step).wait_send()
+    for p, h in pieces:
+        for side in range(2):
+            pl.when(has[side])(move(p, h, side).wait_send)
+            pl.when(has[1 - side])(move(p, h, side).wait_recv)
         real, imag = 0.0, 0.0
+        mine = slice(h * rows_half, (h + 1) * rows_half)
         for side in range(2):
-            source_real = halo[side, p, 0].astype(F32)
-            source_imag = halo[side, p, 1].astype(F32)
-            real = real + (sums[side, 0] * source_real - sums[side, 1] * source_imag)
-            imag = imag + (sums[side, 0] * source_imag + sums[side, 1] * source_real)
-        out_ref[2 * p] = real.astype(BF16)
-        out_ref[2 * p + 1] = imag.astype(BF16)
+            source_real = jnp.where(has[1 - side], halo[side, p, h, 0].astype(F32), 0.0)
+            source_imag = jnp.where(has[1 - side], halo[side, p, h, 1].astype(F32), 0.0)
+            weight_real, weight_imag = sums[side, 0, mine], sums[side, 1, mine]
+            real = real + (weight_real * source_real - weight_imag * source_imag)
+            imag = imag + (weight_real * source_imag + weight_imag * source_real)
+        out_ref[2 * p, mine] = real.astype(BF16)
+        out_ref[2 * p + 1, mine] = imag.astype(BF16)
 
 
 def shards(
@@ -464,16 +491,19 @@
     forward = jnp.asarray(forward_table(length, dirs))
     modes = modes_local // PARTS
     vmem = pl.BlockSpec(memory_space=pltpu.VMEM)
-    smem = pl.BlockSpec(memory_space=pltpu.SMEM)
-    hbm = pl.BlockSpec(memory_space=pl.ANY)
-    inverse = jnp.asarray(inverse_table(length, dirs))
+    hbm = pl.BlockSpec(memory_space=pltpu.HBM)
+    inverse = jnp.asarray(inverse_table(length))
     exchange = pltpu.SemaphoreType.DMA((CHUNKS, dirs - 1))
+    back = pltpu.SemaphoreType.DMA((2, 2, dirs - 1))
     out = pl.pallas_call(
         functools.partial(fused, dirs, boxes),
         out_shape=jax.ShapeDtypeStruct((comps, rows_out, length), BF16),
-        in_specs=[smem] * 3 + [hbm] * 7,
+        in_specs=[hbm] * 10,
         out_specs=vmem,
         scratch_shapes=[
+            pltpu.SMEM(source_list.shape, jnp.int32),
+            pltpu.SMEM(offset_list.shape, jnp.int32),
+            pltpu.SMEM(row_counts.shape, jnp.int32),
             pltpu.VMEM(children.shape[1:], BF16),
             pltpu.VMEM(forward.shape, BF16),
             pltpu.VMEM(axial_angle.shape, F32),
@@ -486,24 +516,24 @@
             pltpu.VMEM((CHUNKS, dirs, 2 * modes, rows // 2), BF16),
             pltpu.VMEM((modes * kids * 2, LANES), F32),
             pltpu.VMEM((theta_out // LANES, 8 * modes, LANES), F32),
-            pltpu.VMEM((CHUNKS, dirs, 4, modes, LANES), BF16),
-            pltpu.VMEM((CHUNKS, 4, length // PARTS, LANES), BF16),
-            pltpu.VMEM((2, LANES, 2 * length), F32),
+            pltpu.VMEM((2, 2, dirs, 2, modes_local, LANES), BF16),
+            pltpu.VMEM((2, 2, 2, length, LANES), BF16),
             pltpu.VMEM(planar_angle.shape, F32),
             pltpu.VMEM(planar_angle.shape, F32),
             pltpu.VMEM((2, 2, rows_out, length), F32),
-            pltpu.VMEM((2, 2, rows_out, length), BF16),
-            pltpu.VMEM((2, 2, 2, rows_out, length), BF16),
+            pltpu.VMEM((2, 2, 2, rows_out // 2, length), BF16),
+            pltpu.VMEM((2, 2, 2, 2, rows_out // 2, length), BF16),
             pltpu.SemaphoreType.DMA((6 + PARTS,)),
+            pltpu.SemaphoreType.DMA((3,)),
             exchange,
             exchange,
-            exchange,
-            exchange,
-            pltpu.SemaphoreType.DMA((2, 2)),
-            pltpu.SemaphoreType.DMA((2, 2)),
+            back,
+            back,
+            pltpu.SemaphoreType.DMA((2, 2, 2)),
+            pltpu.SemaphoreType.DMA((2, 2, 2)),
         ],
         compiler_params=pltpu.CompilerParams(
-            collective_id=0, has_side_effects=True, vmem_limit_bytes=63 * 1024 * 1024
+            collective_id=0, has_side_effects=True, vmem_limit_bytes=60 * 1024 * 1024
         ),
     )(
         source_list,

time: 60.6 us -> 58 us (0.957)
  Pallas kernels: 57.9 us -> 55.2 us
    pallas_call x1, Pallas kernels: 57.9 us -> 55.2 us  [shards(): pl.pallas_call(functools.partial(fused, dirs, boxes), out_shape=jax.Shape...]
where the time goes in v1:
time: 58 us; the launch traced here: 57.8 us
  Pallas kernels  55.2 us (95%)
  local copies, waits for them, and re-layouts  1.86 us (3%)
  between operations  0.66 us (1%)
    pallas_call x1, Pallas kernels, shards(): pl.pallas_call(functools.partial(fused, dirs, boxes), out_shape=jax.Shape...  55.2 us
    broadcast_in_dim x1, local copies, waits for them, and re-layouts, shards(): return out.transpose(1, 0, 2)[None]  1.86 us

profile of v1, /device:TPU:1, one launch (start us, length us, event | category | flops | bytes accessed | tf_op | source)
XLA Modules:
  0.0 57.8 jit_solution(9185717248392334147)
XLA Ops:
  0.7 55.2 %shard_map.100 = bf16[4,64,512]{2,1,0:T(8,128)(2,1)} custom-call(s32[1,8]{1,0:T(1,128)} %source_hbm.1, s32[1,8]{1,0:T(1,128)} %offset_hbm.1, s32[1]{0:T(128)S(6)} %copy.12.count_hbm, bf16[8,32,4,512]{3,2,1,0:T(4,128)(2,1)} %bitcast.5, bf16[2,512,1024]{2,1,0:T(8,128)(2,1)} %constant.4.clone.wf_hbm, f32[2,256]{1,0:T(2,128)} %axial_hbm.1, ...), custom_call_target="tpu_custom_call" | custom-call | tf_op jit(solution)/shard_map/pallas_call | solution.py:498
  55.9 1.9 %copy.11 = bf16[1,64,4,512]{3,2,1,0:T(4,128)(2,1)} copy(bf16[1,64,4,512]{3,1,2,0:T(8,128)(2,1)} %bitcast.4) | data formatting | bytes 524288 | tf_op jit(solution)/shard_map/broadcast_in_dim | solution.py:550

commit v2 on v1

--- a/solution.py
+++ b/solution.py
@@ -533,19 +533,24 @@
             pltpu.SemaphoreType.DMA((2, 2, 2)),
         ],
         compiler_params=pltpu.CompilerParams(
-            collective_id=0, has_side_effects=True, vmem_limit_bytes=60 * 1024 * 1024
+            collective_id=0, has_side_effects=True, vmem_limit_bytes=40 * 1024 * 1024
         ),
     )(
-        source_list,
-        offset_list,
+        pltpu.with_memory_space_constraint(source_list, pltpu.HBM),
+        pltpu.with_memory_space_constraint(offset_list, pltpu.HBM),
         row_counts,
-        children[0],
-        forward,
-        axial_angle,
-        legendre,
-        inverse,
-        planar_angle,
-        translator,
+        *(
+            pltpu.with_memory_space_constraint(item, pltpu.HBM)
+            for item in (
+                children[0],
+                forward,
+                axial_angle,
+                legendre,
+                inverse,
+                planar_angle,
+                translator,
+            )
+        ),
     )
     return out.transpose(1, 0, 2)[None]
 

time: 58 us -> 56.4 us (0.972)
  local copies, waits for them, and re-layouts: 1.86 us -> 0.91 us
  Pallas kernels: 55.2 us -> 54.6 us
    broadcast_in_dim x1, local copies, waits for them, and re-layouts: 1.86 us -> 0.91 us  [shards(): return out.transpose(1, 0, 2)[None]]
    pallas_call x1, Pallas kernels: 55.2 us -> 54.6 us  [shards(): pl.pallas_call(functools.partial(fused, dirs, boxes), out_shape=jax.Shape...]
where the time goes in v2:
time: 56.4 us; the launch traced here: 56.1 us
  Pallas kernels  54.6 us (97%)
  local copies, waits for them, and re-layouts  0.91 us (2%)
  between operations  0.66 us (1%)
    pallas_call x1, Pallas kernels, shards(): pl.pallas_call(functools.partial(fused, dirs, boxes), out_shape=jax.Shape...  54.6 us

profile of v2, /device:TPU:1, one launch (start us, length us, event | category | flops | bytes accessed | tf_op | source)
XLA Modules:
  0.0 56.1 jit_solution(16964089441444208648)
XLA Ops:
  0.7 54.6 %shard_map.100 = bf16[4,64,512]{2,1,0:T(8,128)(2,1)S(1)} custom-call(s32[1,8]{1,0:T(1,128)} %source_hbm.1, s32[1,8]{1,0:T(1,128)} %offset_hbm.1, s32[1]{0:T(128)S(6)} %copy.12.count_hbm, bf16[8,32,4,512]{3,2,1,0:T(4,128)(2,1)} %bitcast.5, bf16[2,512,1024]{2,1,0:T(8,128)(2,1)} %constant.4.clone.wf_hbm, f32[2,256]{1,0:T(2,128)} %axial_hbm.1, ...), custom_call_target="tpu_custom_call" | custom-call | tf_op jit(solution)/shard_map/pallas_call | solution.py:498
  55.2 0.9 %copy.11 = bf16[1,64,4,512]{3,2,1,0:T(4,128)(2,1)} copy(bf16[1,64,4,512]{3,1,2,0:T(8,128)(2,1)S(1)} %bitcast.4) | data formatting | bytes 524288 | tf_op jit(solution)/shard_map/broadcast_in_dim | solution.py:555

commit v3 on v2

--- a/solution.py
+++ b/solution.py
@@ -126,6 +126,8 @@
 
 PARTS = 2
 CHUNKS = 2 * PARTS
+PIECES = 4
+EXCHANGE = 32
 
 
 def forward_table(length, dirs):
@@ -141,10 +143,7 @@
 
 def inverse_table(length):
     phase = np.outer(np.arange(length), np.arange(length)) % length * (2.0 * np.pi / length)
-    cosine, sine = np.cos(phase) / length, np.sin(phase) / length
-    both = np.concatenate(
-        [np.concatenate([cosine, sine], axis=1), np.concatenate([-sine, cosine], axis=1)], axis=0
-    )
+    both = np.concatenate([np.cos(phase) / length, np.sin(phase) / length], axis=1)
     return both.astype(ml_dtypes.bfloat16)
 
 
@@ -179,6 +178,7 @@
     pairs,
     send2,
     recv2,
+    field,
     planar_cos,
     planar_sin,
     sums,
@@ -202,7 +202,14 @@
     rows_in = LANES // dirs
     slots = source_ref.shape[1]
     peers = (me + 1 - 2 * lax.rem(me, 2), lax.rem(me + 2, 4), 3 - me)
-    order = (1, 2, 0)
+    inner = lax.rem((me + 1) // 2, 2)
+
+    def peer_of(step):
+        low = lax.rem(me % 2 + (step + 1) % 2, 2)
+        high = lax.rem(me // 2 + (step + 1) // 2, 2)
+        return low + 2 * high
+
+    second, third = 2 * inner, 2 - 2 * inner
 
     barrier = pltpu.get_barrier_semaphore()
     for peer in peers:
@@ -232,23 +239,23 @@
 
     def out_copy(chunk, step):
         return pltpu.make_async_remote_copy(
-            src_ref=send1.at[chunk, peers[step]],
+            src_ref=send1.at[chunk, peer_of(step)],
             dst_ref=recv1.at[chunk, me],
             send_sem=send1_sems.at[chunk, step],
             recv_sem=recv1_sems.at[chunk, step],
-            device_id=(box, peers[step]),
+            device_id=(box, peer_of(step)),
             device_id_type=MESH,
         )
 
-    place = pl.ds(pl.multiple_of(me * own, own), own)
-
-    def back_copy(p, h, step):
+    def back_copy(p, piece, step):
+        part = slice(None) if p == 0 else piece
+        index = 0 if p == 0 else 1 + piece
         return pltpu.make_async_remote_copy(
-            src_ref=send2.at[p, h, peers[step]],
-            dst_ref=recv2.at[p, h, :, place, :],
-            send_sem=send2_sems.at[p, h, step],
-            recv_sem=recv2_sems.at[p, h, step],
-            device_id=(box, peers[step]),
+            src_ref=send2.at[p, peer_of(step), part],
+            dst_ref=recv2.at[p, me, part],
+            send_sem=send2_sems.at[index, step],
+            recv_sem=recv2_sems.at[index, step],
+            device_id=(box, peer_of(step)),
             device_id_type=MESH,
         )
 
@@ -269,27 +276,39 @@
             ]
     cols = samples.shape[0] // 2
 
+    def transform(table, p):
+        return lax.dot_general(
+            table,
+            samples[p * cols : (p + 1) * cols],
+            (((1,), (1,)), ((), ())),
+            preferred_element_type=F32,
+        ).astype(BF16)
+
     for chunk in range(CHUNKS):
         p, part = chunk // PARTS, chunk % PARTS
         if p == 0:
             load_wf[part].wait()
-        spectrum = lax.dot_general(
-            wf_ref[part],
-            samples[p * cols : (p + 1) * cols],
-            (((1,), (1,)), ((), ())),
-            preferred_element_type=F32,
-        )
-        send1[chunk] = spectrum.astype(BF16).reshape(send1.shape[1:])
         if chunk == 0:
-            pl.semaphore_wait(barrier, dirs + 1)
-        out_copy(chunk, 1).start()
-        out_copy(chunk, 2).start()
+            targets = (peers[1], peer_of(second), peer_of(third), me)
+            for i, target in enumerate(targets):
+                tall = 2 * modes
+                send1[chunk, target] = transform(
+                    wf_ref[part, pl.ds(pl.multiple_of(target * tall, tall), tall)], p
+                )
+                if i == 0:
+                    pl.semaphore_wait(barrier, dirs + 1)
+                if i < 2:
+                    out_copy(chunk, (1, second)[i]).start()
+        else:
+            send1[chunk] = transform(wf_ref[part], p).reshape(send1.shape[1:])
+            out_copy(chunk, 1).start()
+            out_copy(chunk, second).start()
         if chunk == 0:
             for item in (load_planar, *load_index, load_translator, load_axial, load_legendre, load_wi):
                 item.start()
         if part == PARTS - 1:
             for i in range(PARTS):
-                out_copy(p * PARTS + i, 0).start()
+                out_copy(p * PARTS + i, third).start()
         recv1[chunk, me] = send1[chunk, me]
 
     load_planar.wait()
@@ -321,6 +340,7 @@
     angle = jnp.where(upper, axial_ref[0:1], axial_ref[1:2])
     axial_cos, axial_sin = jnp.cos(angle), jnp.sin(angle)
     block = lax.broadcasted_iota(jnp.int32, (modes, LANES), 1) // rows_in
+    lane = lax.broadcasted_iota(jnp.int32, (EXCHANGE, LANES), 1)
     load_legendre.wait()
 
     def exchanged(tiles, a):
@@ -371,14 +391,22 @@
             return inner
 
         lax.fori_loop(0, modes, mode, 0, unroll=8)
-        rows = pl.ds(pl.multiple_of(first, modes), modes)
         for n in range(pairs.shape[0]):
-            for r in range(2):
-                tiles = [
-                    pairs[n, (r * 4 + q) * modes : (r * 4 + q + 1) * modes, :] for q in range(4)
-                ]
-                for g in range(4):
-                    send2[p, g % 2, 2 * n + g // 2, r, rows] = exchanged(tiles, g).astype(BF16)
+            for top in range(0, modes, EXCHANGE):
+                tiles = [pairs[n, k * modes + top : k * modes + top + EXCHANGE, :] for k in range(8)]
+                for bit in (1, 2, 4):
+                    distance = bit * LANES // 8
+                    for k in range(8):
+                        if not k & bit:
+                            one, two = tiles[k], tiles[k | bit]
+                            clear = lane // distance % 2 == 0
+                            tiles[k] = jnp.where(clear, one, pltpu.roll(two, distance, 1))
+                            tiles[k | bit] = jnp.where(
+                                clear, pltpu.roll(one, LANES - distance, 1), two
+                            )
+                rows = pl.ds(pl.multiple_of(first + top, EXCHANGE), EXCHANGE)
+                for g in range(8):
+                    send2[p, 2 * n + g // 4, g % 4, rows] = tiles[g].astype(BF16)
 
     for p in range(2):
 
@@ -387,66 +415,77 @@
             return carry
 
         lax.fori_loop(0, PARTS, both_parts, 0)
-        for h, step in ((0, 1), (1, 1), (0, 2), (1, 2), (0, 0), (1, 0)):
-            back_copy(p, h, step).start()
-        for h in range(2):
-            recv2[p, h, :, place, :] = send2[p, h, me]
+        for step in (1, second, third):
+            for piece in range(1 if p == 0 else PIECES):
+                back_copy(p, piece, step).start()
+        recv2[p, me] = send2[p, me]
 
     load_wi.wait()
     has = (box < boxes - 1, box > 0)
-
-    def move(p, h, side):
+    far = 1 - lax.rem(box, 2)
+
+    def move(p, piece, side):
+        part = slice(None) if p == 0 else piece
+        index = 0 if p == 0 else 1 + piece
         return pltpu.make_async_remote_copy(
-            src_ref=stored.at[p, h],
-            dst_ref=halo.at[side, p, h],
-            send_sem=halo_send.at[side, p, h],
-            recv_sem=halo_recv.at[side, p, h],
-            device_id=((right, left)[side], me),
+            src_ref=stored.at[p, part],
+            dst_ref=halo.at[side, p, part],
+            send_sem=halo_send.at[side, index],
+            recv_sem=halo_recv.at[side, index],
+            device_id=(box + 1 - 2 * side, me),
             device_id_type=MESH,
         )
 
-    rows_half = rows_out // 2
-    pieces = [(p, h) for p in range(2) for h in range(2)]
-    for p, h in pieces:
-        for step in range(3):
-            back_copy(p, h, step).wait_recv()
-        field = lax.dot_general(
-            recv2[p, h].reshape(-1, LANES),
-            wi_ref[...],
-            (((0,), (0,)), ((), ())),
-            preferred_element_type=F32,
-        )
-        total_real, total_imag = 0.0, 0.0
-        for q in range(4):
-            cos = planar_cos[q, h * rows_half : (h + 1) * rows_half]
-            sin = planar_sin[q, h * rows_half : (h + 1) * rows_half]
-            real = field[q * rows_half : (q + 1) * rows_half, :length]
-            imag = field[q * rows_half : (q + 1) * rows_half, length:]
-            total_real = total_real + (real * cos - imag * sin)
-            total_imag = total_imag + (real * sin + imag * cos)
-        stored[p, h, 0] = total_real.astype(BF16)
-        stored[p, h, 1] = total_imag.astype(BF16)
-        for side in range(2):
-            pl.when(has[side])(move(p, h, side).start)
+    band = rows_out // PIECES
+    for p in range(2):
+        for piece in range(PIECES):
+            if p == 1 or piece == 0:
+                for step in range(3):
+                    back_copy(p, piece, step).wait_recv()
+            field[...] = lax.dot_general(
+                recv2[p, :, piece].reshape(-1, LANES),
+                wi_ref[...],
+                (((0,), (0,)), ((), ())),
+                preferred_element_type=F32,
+            )
+            total_real, total_imag = 0.0, 0.0
+            for q in range(4):
+                cos = planar_cos[q, piece * band : (piece + 1) * band]
+                sin = planar_sin[q, piece * band : (piece + 1) * band]
+                one = field[q * band : (q + 1) * band]
+                two = field[(4 + q) * band : (5 + q) * band]
+                real = one[:, :length] - two[:, length:]
+                imag = one[:, length:] + two[:, :length]
+                total_real = total_real + (real * cos - imag * sin)
+                total_imag = total_imag + (real * sin + imag * cos)
+            stored[p, piece, 0] = total_real.astype(BF16)
+            stored[p, piece, 1] = total_imag.astype(BF16)
+            if p == 1 or piece == PIECES - 1:
+                for side in (far, 1 - far):
+                    there = box + 1 - 2 * side
+                    pl.when(jnp.logical_and(there >= 0, there < boxes))(move(p, piece, side).start)
     for step in range(3):
         for chunk in range(CHUNKS):
             out_copy(chunk, step).wait_send()
-        for p, h in pieces:
-            back_copy(p, h, step).wait_send()
-    for p, h in pieces:
-        for side in range(2):
-            pl.when(has[side])(move(p, h, side).wait_send)
-            pl.when(has[1 - side])(move(p, h, side).wait_recv)
-        real, imag = 0.0, 0.0
-        mine = slice(h * rows_half, (h + 1) * rows_half)
-        for side in range(2):
-            source_real = jnp.where(has[1 - side], halo[side, p, h, 0].astype(F32), 0.0)
-            source_imag = jnp.where(has[1 - side], halo[side, p, h, 1].astype(F32), 0.0)
-            weight_real, weight_imag = sums[side, 0, mine], sums[side, 1, mine]
-            real = real + (weight_real * source_real - weight_imag * source_imag)
-            imag = imag + (weight_real * source_imag + weight_imag * source_real)
-        out_ref[2 * p, mine] = real.astype(BF16)
-        out_ref[2 * p + 1, mine] = imag.astype(BF16)
+        for piece in range(PIECES):
+            back_copy(1, piece, step).wait_send()
+        back_copy(0, 0, step).wait_send()
+    for p in range(2):
+        for piece in range(PIECES):
+            if p == 1 or piece == 0:
+                for side in range(2):
+                    pl.when(has[side])(move(p, piece, side).wait_send)
+                    pl.when(has[1 - side])(move(p, piece, side).wait_recv)
+            real, imag = 0.0, 0.0
+            mine = slice(piece * band, (piece + 1) * band)
+            for side in range(2):
+                source_real = jnp.where(has[1 - side], halo[side, p, piece, 0].astype(F32), 0.0)
+                source_imag = jnp.where(has[1 - side], halo[side, p, piece, 1].astype(F32), 0.0)
+                weight_real, weight_imag = sums[side, 0, mine], sums[side, 1, mine]
+                real = real + (weight_real * source_real - weight_imag * source_imag)
+                imag = imag + (weight_real * source_imag + weight_imag * source_real)
+            out_ref[2 * p, mine] = real.astype(BF16)
+            out_ref[2 * p + 1, mine] = imag.astype(BF16)
 
 
 def shards(
@@ -473,6 +512,7 @@
         and comps == 4
         and theta_in == LANES
         and 2 * rows_out == LANES
+        and rows_out % (16 * PIECES) == 0
         and modes_local == LANES
     )
     if not fits:
@@ -494,7 +534,7 @@
     hbm = pl.BlockSpec(memory_space=pltpu.HBM)
     inverse = jnp.asarray(inverse_table(length))
     exchange = pltpu.SemaphoreType.DMA((CHUNKS, dirs - 1))
-    back = pltpu.SemaphoreType.DMA((2, 2, dirs - 1))
+    back = pltpu.SemaphoreType.DMA((1 + PIECES, dirs - 1))
     out = pl.pallas_call(
         functools.partial(fused, dirs, boxes),
         out_shape=jax.ShapeDtypeStruct((comps, rows_out, length), BF16),
@@ -516,21 +556,22 @@
             pltpu.VMEM((CHUNKS, dirs, 2 * modes, rows // 2), BF16),
             pltpu.VMEM((modes * kids * 2, LANES), F32),
             pltpu.VMEM((theta_out // LANES, 8 * modes, LANES), F32),
-            pltpu.VMEM((2, 2, dirs, 2, modes_local, LANES), BF16),
-            pltpu.VMEM((2, 2, 2, length, LANES), BF16),
+            pltpu.VMEM((2, dirs, PIECES, modes_local, LANES), BF16),
+            pltpu.VMEM((2, dirs, PIECES, modes_local, LANES), BF16),
+            pltpu.VMEM((LANES, 2 * length), F32),
             pltpu.VMEM(planar_angle.shape, F32),
             pltpu.VMEM(planar_angle.shape, F32),
             pltpu.VMEM((2, 2, rows_out, length), F32),
-            pltpu.VMEM((2, 2, 2, rows_out // 2, length), BF16),
-            pltpu.VMEM((2, 2, 2, 2, rows_out // 2, length), BF16),
+            pltpu.VMEM((2, PIECES, 2, rows_out // PIECES, length), BF16),
+            pltpu.VMEM((2, 2, PIECES, 2, rows_out // PIECES, length), BF16),
             pltpu.SemaphoreType.DMA((6 + PARTS,)),
             pltpu.SemaphoreType.DMA((3,)),
             exchange,
             exchange,
             back,
             back,
-            pltpu.SemaphoreType.DMA((2, 2, 2)),
-            pltpu.SemaphoreType.DMA((2, 2, 2)),
+            pltpu.SemaphoreType.DMA((2, 1 + PIECES)),
+            pltpu.SemaphoreType.DMA((2, 1 + PIECES)),
         ],
         compiler_params=pltpu.CompilerParams(
             collective_id=0, has_side_effects=True, vmem_limit_bytes=40 * 1024 * 1024

time: 56.4 us -> 55.6 us (0.986)
  Pallas kernels: 54.6 us -> 53.7 us
    pallas_call x1, Pallas kernels: 54.6 us -> 53.7 us  [shards(): pl.pallas_call(functools.partial(fused, dirs, boxes), out_shape=jax.Shape...]
where the time goes in v3:
time: 55.6 us; the launch traced here: 55.3 us
  Pallas kernels  53.7 us (97%)
  local copies, waits for them, and re-layouts  0.91 us (2%)
  between operations  0.66 us (1%)
    pallas_call x1, Pallas kernels, shards(): pl.pallas_call(functools.partial(fused, dirs, boxes), out_shape=jax.Shape...  53.7 us

profile of v3, /device:TPU:1, one launch (start us, length us, event | category | flops | bytes accessed | tf_op | source)
XLA Modules:
  0.0 55.3 jit_solution(10304433507553560501)
XLA Ops:
  0.7 53.7 %shard_map.100 = bf16[4,64,512]{2,1,0:T(8,128)(2,1)S(1)} custom-call(s32[1,8]{1,0:T(1,128)} %source_hbm.1, s32[1,8]{1,0:T(1,128)} %offset_hbm.1, s32[1]{0:T(128)S(6)} %copy.12.count_hbm, bf16[8,32,4,512]{3,2,1,0:T(4,128)(2,1)} %bitcast.5, bf16[2,512,1024]{2,1,0:T(8,128)(2,1)} %constant.4.clone.wf_hbm, f32[2,256]{1,0:T(2,128)} %axial_hbm.1, ...), custom_call_target="tpu_custom_call" | custom-call | tf_op jit(solution)/shard_map/pallas_call | solution.py:538
  54.4 0.9 %copy.11 = bf16[1,64,4,512]{3,2,1,0:T(4,128)(2,1)} copy(bf16[1,64,4,512]{3,1,2,0:T(8,128)(2,1)S(1)} %bitcast.4) | data formatting | bytes 524288 | tf_op jit(solution)/shard_map/broadcast_in_dim | solution.py:596

commit v4 on v3

--- a/solution.py
+++ b/solution.py
@@ -184,6 +184,7 @@
     sums,
     stored,
     halo,
+    flat,
     local_sems,
     index_sems,
     send1_sems,
@@ -195,7 +196,7 @@
 ):
     me = lax.axis_index("dir")
     box = lax.axis_index("box")
-    right, left = lax.rem(box + 1, boxes), lax.rem(box + boxes - 1, boxes)
+    ends = (boxes - box) // boxes + (box + 1) // boxes
     rows_out, length = planar_ref.shape[1:]
     own = legendre_ref.shape[0]
     modes = own // PARTS
@@ -214,15 +215,26 @@
     barrier = pltpu.get_barrier_semaphore()
     for peer in peers:
         pl.semaphore_signal(barrier, inc=1, device_id=(box, peer), device_id_type=MESH)
-    for peer in (left, right):
-        pl.semaphore_signal(barrier, inc=1, device_id=(peer, me), device_id_type=MESH)
+    for peer, there in ((box - 1, box > 0), (box + 1, box < boxes - 1)):
+
+        @pl.when(there)
+        def _(peer=peer):
+            pl.semaphore_signal(barrier, inc=1, device_id=(peer, me), device_id_type=MESH)
+
 
     def load(src, dst, sem):
         return pltpu.make_async_copy(src, dst, sem)
 
     load_x = load(x_hbm, x_ref, local_sems.at[0])
-    load_wf = [load(wf_hbm.at[i], wf_ref.at[i], local_sems.at[1 + i]) for i in range(PARTS)]
-    at = 1 + PARTS
+    tall = wf_ref.shape[1] // dirs
+    targets = (peers[1], peer_of(second), peer_of(third), me)
+    bands = [pl.ds(pl.multiple_of(target * tall, tall), tall) for target in targets]
+    load_first = [
+        load(wf_hbm.at[0, bands[i]], wf_ref.at[0, bands[i]], local_sems.at[1 + i])
+        for i in range(dirs)
+    ]
+    load_wf = load(wf_hbm.at[1], wf_ref.at[1], local_sems.at[1 + dirs])
+    at = 2 + dirs
     load_planar = load(planar_hbm, planar_ref, local_sems.at[at])
     load_translator = load(translator_hbm, translator_ref, local_sems.at[at + 1])
     load_legendre = load(legendre_hbm, legendre_ref, local_sems.at[at + 2])
@@ -234,7 +246,7 @@
             ((source_hbm, source_ref), (offset_hbm, offset_ref), (count_hbm, count_ref))
         )
     ]
-    for item in (load_x, *load_wf):
+    for item in (load_x, *load_first, load_wf):
         item.start()
 
     def out_copy(chunk, step):
@@ -286,17 +298,16 @@
 
     for chunk in range(CHUNKS):
         p, part = chunk // PARTS, chunk % PARTS
-        if p == 0:
-            load_wf[part].wait()
+        if chunk == 1:
+            load_wf.wait()
         if chunk == 0:
-            targets = (peers[1], peer_of(second), peer_of(third), me)
             for i, target in enumerate(targets):
-                tall = 2 * modes
+                load_first[i].wait()
                 send1[chunk, target] = transform(
-                    wf_ref[part, pl.ds(pl.multiple_of(target * tall, tall), tall)], p
+                    wf_ref[part, bands[i]], p
                 )
                 if i == 0:
-                    pl.semaphore_wait(barrier, dirs + 1)
+                    pl.semaphore_wait(barrier, dirs + 1 - ends)
                 if i < 2:
                     out_copy(chunk, (1, second)[i]).start()
         else:
@@ -437,6 +448,9 @@
         )
 
     band = rows_out // PIECES
+    into = lax.broadcasted_iota(jnp.int32, (4 * band, 4 * band), 0)
+    outof = lax.broadcasted_iota(jnp.int32, (4 * band, 4 * band), 1)
+    final = ((into % 4) * band + into // 4 == outof).astype(F32).astype(BF16)
     for p in range(2):
         for piece in range(PIECES):
             if p == 1 or piece == 0:
@@ -484,8 +498,11 @@
                 weight_real, weight_imag = sums[side, 0, mine], sums[side, 1, mine]
                 real = real + (weight_real * source_real - weight_imag * source_imag)
                 imag = imag + (weight_real * source_imag + weight_imag * source_real)
-            out_ref[2 * p, mine] = real.astype(BF16)
-            out_ref[2 * p + 1, mine] = imag.astype(BF16)
+            flat[piece, 2 * p * band : (2 * p + 1) * band] = real.astype(BF16)
+            flat[piece, (2 * p + 1) * band : (2 * p + 2) * band] = imag.astype(BF16)
+            if p == 1:
+                mixed = jnp.dot(final, flat[piece], preferred_element_type=F32).astype(BF16)
+                out_ref[mine] = mixed.reshape(band, 4, length)
 
 
 def shards(
@@ -537,7 +554,7 @@
     back = pltpu.SemaphoreType.DMA((1 + PIECES, dirs - 1))
     out = pl.pallas_call(
         functools.partial(fused, dirs, boxes),
-        out_shape=jax.ShapeDtypeStruct((comps, rows_out, length), BF16),
+        out_shape=jax.ShapeDtypeStruct((rows_out, comps, length), BF16),
         in_specs=[hbm] * 10,
         out_specs=vmem,
         scratch_shapes=[
@@ -564,7 +581,8 @@
             pltpu.VMEM((2, 2, rows_out, length), F32),
             pltpu.VMEM((2, PIECES, 2, rows_out // PIECES, length), BF16),
             pltpu.VMEM((2, 2, PIECES, 2, rows_out // PIECES, length), BF16),
-            pltpu.SemaphoreType.DMA((6 + PARTS,)),
+            pltpu.VMEM((PIECES, comps * rows_out // PIECES, length), BF16),
+            pltpu.SemaphoreType.DMA((7 + dirs,)),
             pltpu.SemaphoreType.DMA((3,)),
             exchange,
             exchange,
@@ -593,7 +611,7 @@
             )
         ),
     )
-    return out.transpose(1, 0, 2)[None]
+    return out[None]
 
 
 def solution(mesh):

time: 55.6 us -> 55.6 us (level)
    broadcast_in_dim x1 -> x0, local copies, waits for them, and re-layouts: 0.91 us -> none  [shards(): return out.transpose(1, 0, 2)[None]]
    unnamed x0 -> x1, local copies, waits for them, and re-layouts: none -> 0.71 us
where the time goes in v4:
time: 55.6 us; the launch traced here: 55.3 us
  Pallas kernels  53.9 us (97%)
  local copies, waits for them, and re-layouts  0.71 us (1%)
  between operations  0.66 us (1%)
    pallas_call x1, Pallas kernels, shards(): pl.pallas_call(functools.partial(fused, dirs, boxes), out_shape=jax.Shape...  53.9 us

profile of v4, /device:TPU:1, one launch (start us, length us, event | category | flops | bytes accessed | tf_op | source)
XLA Modules:
  0.0 55.3 jit_solution(15666508240529970076)
XLA Ops:
  0.7 53.9 %shard_map.100 = bf16[64,4,512]{2,1,0:T(4,128)(2,1)S(1)} custom-call(s32[1,8]{1,0:T(1,128)} %source_hbm.1, s32[1,8]{1,0:T(1,128)} %offset_hbm.1, s32[1]{0:T(128)S(6)} %copy.12.count_hbm, bf16[8,32,4,512]{3,2,1,0:T(4,128)(2,1)} %bitcast.3, bf16[2,512,1024]{2,1,0:T(8,128)(2,1)} %constant.4.clone.wf_hbm, f32[2,256]{1,0:T(2,128)} %axial_hbm.1, ...), custom_call_target="tpu_custom_call" | custom-call | tf_op jit(solution)/shard_map/pallas_call | solution.py:555
  54.6 0.7 %copy.13 = bf16[1,64,4,512]{3,2,1,0:T(4,128)(2,1)} copy(bf16[1,64,4,512]{3,2,1,0:T(4,128)(2,1)S(1)} %bitcast.2) | data formatting | bytes 524288

commit v5 on v4

--- a/solution.py
+++ b/solution.py
@@ -475,9 +475,11 @@
             stored[p, piece, 0] = total_real.astype(BF16)
             stored[p, piece, 1] = total_imag.astype(BF16)
             if p == 1 or piece == PIECES - 1:
-                for side in (far, 1 - far):
-                    there = box + 1 - 2 * side
-                    pl.when(jnp.logical_and(there >= 0, there < boxes))(move(p, piece, side).start)
+                there = box + 1 - 2 * far
+                pl.when(jnp.logical_and(there >= 0, there < boxes))(move(p, piece, far).start)
+                if piece == PIECES - 1:
+                    for item in range(PIECES if p else 1):
+                        move(p, item, 1 - far).start()
     for step in range(3):
         for chunk in range(CHUNKS):
             out_copy(chunk, step).wait_send()

time: 55.6 us -> 55.6 us (level)
  no operation moved by 1% of the time
where the time goes in v5:
time: 55.6 us; the launch traced here: 55.3 us
  Pallas kernels  53.9 us (97%)
  local copies, waits for them, and re-layouts  0.71 us (1%)
  between operations  0.66 us (1%)
    pallas_call x1, Pallas kernels, shards(): pl.pallas_call(functools.partial(fused, dirs, boxes), out_shape=jax.Shape...  53.9 us

profile of v5, /device:TPU:1, one launch (start us, length us, event | category | flops | bytes accessed | tf_op | source)
XLA Modules:
  0.0 55.3 jit_solution(17358716935372524284)
XLA Ops:
  0.7 53.9 %shard_map.100 = bf16[64,4,512]{2,1,0:T(4,128)(2,1)S(1)} custom-call(s32[1,8]{1,0:T(1,128)} %source_hbm.1, s32[1,8]{1,0:T(1,128)} %offset_hbm.1, s32[1]{0:T(128)S(6)} %copy.12.count_hbm, bf16[8,32,4,512]{3,2,1,0:T(4,128)(2,1)} %bitcast.3, bf16[2,512,1024]{2,1,0:T(8,128)(2,1)} %constant.4.clone.wf_hbm, f32[2,256]{1,0:T(2,128)} %axial_hbm.1, ...), custom_call_target="tpu_custom_call" | custom-call | tf_op jit(solution)/shard_map/pallas_call | solution.py:557
  54.6 0.7 %copy.13 = bf16[1,64,4,512]{3,2,1,0:T(4,128)(2,1)} copy(bf16[1,64,4,512]{3,2,1,0:T(4,128)(2,1)S(1)} %bitcast.2) | data formatting | bytes 524288
